TPU v7x, 32 devices: a whole 2x2x4 slice. The times are simulated.
32 devices in a mesh: row: 8 (over z, y), col: 4 (over x, core).
Axes of the slice: x: 2, y: 2, z: 4, core: 2. Of those that a mesh axis runs over, the one named last changes fastest.
Arguments:
- density: float32 [2, 160, 32, 160, 160], P(None, 'col', None, 'row'), may hold values from -2 to 2
- potential: float32 [160, 160], P('row'), may hold values from 0 to 2
Outputs:
- liouville: float32 [2, 160, 160, 1024], P(None, 'col', 'row')
All inputs are finite; a program needn't handle non-finite values.
Results may differ from a plain program's by a relative error of at most 0.000055.
Values sent between devices are 32-bit elements; how exact they have to be, the bound alone decides.
A program may use at most 384 MiB of HBM per device.

v0:
```python
import jax
import jax.numpy as jnp
from jax import lax
from jax.sharding import PartitionSpec as P

friction = 0.005
diffusion = 0.0001
highest = lax.Precision.HIGHEST


def operators(grid_width):
    positions = jnp.arange(grid_width)
    signed = jnp.where(positions < grid_width // 2, positions, positions - grid_width)
    wavenumber = 2.0 * jnp.pi / grid_width * signed.astype(jnp.float32)
    slope_wave = jnp.where(positions == grid_width // 2, 0.0, wavenumber)
    phases = positions[:, None] * positions[None, :] % grid_width
    angles = 2.0 * jnp.pi / grid_width * phases.astype(jnp.float32)
    kinetic_row = jnp.sum(0.5 * wavenumber * wavenumber * jnp.cos(angles), axis=1) / grid_width
    slope_row = -jnp.sum(slope_wave * jnp.sin(angles), axis=1) / grid_width
    distance = (positions[:, None] - positions[None, :]) % grid_width
    return (kinetic_row[distance], slope_row[distance])


def on_device(density, potential):
    grid_width = density.shape[4]
    window_size = density.shape[2]
    cols_here = density.shape[1]
    rows_here = density.shape[3]
    kinetic, slope_matrix = operators(grid_width)
    matrices = jnp.concatenate([kinetic[:window_size].T, slope_matrix[:window_size].T], axis=1)
    product = jnp.einsum("cpqbx,xe->cpebq", density, matrices, precision=highest)
    kinetic_one = product[:, :, :window_size]
    grad_one = product[:, :, window_size:]
    window_part = jnp.transpose(density[..., :window_size], (0, 1, 4, 3, 2))
    local_potential = potential[:, :window_size].T.reshape(1, 1, window_size, rows_here, 1)
    applied = kinetic_one + local_potential * window_part
    stacked = jnp.concatenate([kinetic, slope_matrix], axis=0)
    row_start = lax.axis_index("row") * rows_here
    col_start = lax.axis_index("col") * cols_here
    offset_one = (jnp.arange(window_size)[:, None] - jnp.arange(window_size)[None, :]).astype(
        jnp.float32
    )
    offset_one = offset_one.reshape(1, 1, window_size, 1, window_size)
    rows_global = (
        (row_start + jnp.arange(rows_here)).astype(jnp.float32).reshape(1, 1, 1, rows_here, 1)
    )
    cols_global = (
        (col_start + jnp.arange(cols_here)).astype(jnp.float32).reshape(1, cols_here, 1, 1, 1)
    )
    offset_two = rows_global - cols_global
    squared = offset_one**2 + offset_two**2
    source = lax.all_to_all(window_part, "row", split_axis=2, concat_axis=3, tiled=True)
    applied_mid = lax.all_to_all(applied, "row", split_axis=2, concat_axis=3, tiled=True)
    grad_mid = lax.all_to_all(grad_one, "row", split_axis=2, concat_axis=3, tiled=True)
    paired = jnp.einsum("capbq,eb->capeq", source, stacked, precision=highest)
    full_applied = applied_mid + paired[:, :, :, :grid_width]
    grad_two = paired[:, :, :, grid_width:]
    applied_back, grad_back = (
        lax.all_to_all(full_applied, "row", split_axis=3, concat_axis=2, tiled=True),
        lax.all_to_all(grad_two, "row", split_axis=3, concat_axis=2, tiled=True),
    )
    mirror_applied, mirror_one, mirror_two = (
        lax.all_to_all(
            lax.all_to_all(full_applied, "col", split_axis=3, concat_axis=1, tiled=True),
            "row",
            split_axis=1,
            concat_axis=2,
            tiled=True,
        ),
        lax.all_to_all(
            lax.all_to_all(grad_mid, "col", split_axis=3, concat_axis=1, tiled=True),
            "row",
            split_axis=1,
            concat_axis=2,
            tiled=True,
        ),
        lax.all_to_all(
            lax.all_to_all(grad_two, "col", split_axis=3, concat_axis=1, tiled=True),
            "row",
            split_axis=1,
            concat_axis=2,
            tiled=True,
        ),
    )
    mirror_applied = jnp.transpose(mirror_applied, (0, 3, 4, 1, 2))
    mirror_one = jnp.transpose(mirror_one, (0, 3, 4, 1, 2))
    mirror_two = jnp.transpose(mirror_two, (0, 3, 4, 1, 2))
    differ_real = applied_back[0] - mirror_applied[0]
    differ_imag = applied_back[1] + mirror_applied[1]
    first_real = grad_one[0] - mirror_one[0]
    first_imag = grad_one[1] + mirror_one[1]
    second_real = grad_back[0] - mirror_two[0]
    second_imag = grad_back[1] + mirror_two[1]
    real_out = differ_imag - friction * (offset_one[0] * first_real + offset_two[0] * second_real)
    imag_out = -differ_real - friction * (offset_one[0] * first_imag + offset_two[0] * second_imag)
    real_out = real_out - diffusion * squared[0] * window_part[0]
    imag_out = imag_out - diffusion * squared[0] * window_part[1]
    result = jnp.stack([real_out, imag_out])
    result = jnp.transpose(result, (0, 1, 3, 4, 2))
    return result.reshape(2, cols_here, rows_here, window_size * window_size)


def solution(mesh):
    in_specs = (P(None, "col", None, "row", None), P("row", None))
    out_specs = P(None, "col", "row", None)
    return jax.shard_map(
        on_device, mesh=mesh, in_specs=in_specs, out_specs=out_specs, check_vma=False
    )
```

profile of v0, /device:TPU:0, one launch (start us, length us, event | category | flops | bytes accessed | tf_op | source)
XLA Modules:
  0.0 2895.3 jit_solution(5164920676413358979)
XLA Ops:
  0.1 46.7 %copy.127 = f32[2,40,32,20,160]{4,1,3,2,0:T(8,128)} copy(f32[2,40,32,20,160]{4,2,3,1,0:T(8,128)} %param.2) | data formatting | bytes 65536000 | tf_op args[0]
  47.8 158.1 %gather_fusion.1 = f32[25600]{0:T(1024)S(1)} fusion(f32[160]{0:T(256)S(1)} %negate_multiply_fusion, s32[25600]{0:T(1024)S(1)} %broadcast_clamp_fusion), kind=kCustom, calls=%fused_computation.1 | custom fusion | bytes 307200 | tf_op jit(solution)/shard_map/gather | solution.py:21
  206.7 158.1 %gather_fusion = f32[25600]{0:T(1024)S(1)} fusion(f32[160]{0:T(256)S(1)} %broadcast_multiply_fusion, s32[25600]{0:T(1024)S(1)} %broadcast_clamp_fusion), kind=kCustom, calls=%fused_computation | custom fusion | bytes 307200 | tf_op jit(solution)/shard_map/gather | solution.py:21
  365.0 75.3 %convolution_bitcast_fusion = f32[2,40,64,20,32]{2,1,3,4,0:T(8,128)} fusion(f32[160,32]{0,1:T(8,128)S(1)} %bitcast.148, f32[160,32]{0,1:T(8,128)S(1)} %bitcast.149, f32[2,40,32,20,160]{4,2,3,1,0:T(8,128)} %param.2), kind=kOutput, calls=%fused_computation.10 | convolution fusion | flops 6291466240 | bytes 45916160 | tf_op jit(solution)/shard_map/cpqbx,xe->cpebq/dot_general | solution.py:31
  440.2 43.1 %slice_add_fusion = (f32[2,40,32,20,32]{2,1,3,4,0:T(8,128)}, f32[2,40,32,20,32]{2,1,3,4,0:T(8,128)}) fusion(f32[2,40,64,20,32]{2,1,3,4,0:T(8,128)} %convolution_bitcast_fusion, f32[32,20]{0,1:T(8,128)S(1)} %slice_bitcast_fusion.1, f32[2,40,32,20,160]{4,1,3,2,0:T(8,128)} %copy.127), kind=kLoop, calls=%fused_computation.3 | loop fusion | flops 3276800 | bytes 32770560 | tf_op jit(solution)/shard_map/add | solution.py:36
  483.3 24.2 copy.129
  555.4 24.1 copy.134
  602.4 79.3 %all-to-all-done = f32[8,1,204800]{2,1,0:T(1,128)} async-done(((f32[8,1,204800]{2,1,0:T(1,128)}), f32[8,1,204800]{2,1,0:T(1,128)}, u32[]{:S(2)}, u32[]{:S(2)}) %all-to-all-start) | async-done | bytes 6553632 | tf_op jit(solution)/shard_map/all_to_all | solution.py:53
  686.5 24.1 copy.148
  733.6 95.8 %all-to-all-done.1 = f32[8,1,204800]{2,1,0:T(1,128)} async-done(((f32[8,1,204800]{2,1,0:T(1,128)}), f32[8,1,204800]{2,1,0:T(1,128)}, u32[]{:S(2)}, u32[]{:S(2)}) %all-to-all-start.1) | async-done | bytes 6553632 | tf_op jit(solution)/shard_map/all_to_all | solution.py:52
  835.1 57.0 %reduce = f32[8,204800]{1,0:T(8,128)} reduce(f32[8,1,204800]{2,1,0:T(1,128)} %all-to-all-done, f32[]{:T(128)} %broadcast.227), dimensions={1}, to_apply=%all_to_all.139.reduce_sub_computation | reduce | bytes 13107204 | tf_op jit(solution)/shard_map/all_to_all | solution.py:53
  892.1 26.9 reshape.237
  955.4 57.0 %reduce.1 = f32[8,204800]{1,0:T(8,128)} reduce(f32[8,1,204800]{2,1,0:T(1,128)} %all-to-all-done.1, f32[]{:T(128)} %broadcast.227), dimensions={1}, to_apply=%all_to_all.143.reduce_sub_computation | reduce | bytes 13107204 | tf_op jit(solution)/shard_map/all_to_all | solution.py:52
  1012.4 26.9 reshape.223
  1049.4 43.6 %fusion.15 = f32[2,40,4,320,32]{3,1,4,2,0:T(8,128)} fusion(f32[2,40,4,160,32]{1,4,3,2,0:T(8,128)S(1)} %bitcast.113, f32[160,160]{0,1:T(8,128)S(1)} %copy.133, f32[160,160]{0,1:T(8,128)S(1)} %copy.132), kind=kOutput, calls=%fused_computation.34 | convolution fusion | flops 6291507200 | bytes 19865600 | tf_op jit(solution)/shard_map/capbq,eb->capeq/dot_general | solution.py:55
  1128.3 33.5 %reshape.226 = f32[4,1,409600]{2,1,0:T(1,128)} reshape(f32[160,2,4,32,40]{4,3,2,1,0:T(8,128)} %bitcast.109) | data formatting | bytes 13107200
  1167.2 56.9 %reduce.5 = f32[8,204800]{1,0:T(8,128)} reduce(f32[8,1,204800]{2,1,0:T(1,128)} %all-to-all-done.5, f32[]{:T(128)} %broadcast.227), dimensions={1}, to_apply=%all_to_all.158.reduce_sub_computation | reduce | bytes 13107204 | tf_op jit(solution)/shard_map/all_to_all | solution.py:54
  1224.0 26.9 reshape.231
  1268.2 33.5 %reshape.232 = f32[4,1,409600]{2,1,0:T(1,128)} reshape(f32[160,2,4,32,40]{4,3,2,1,0:T(8,128)} %bitcast.126) | data formatting | bytes 13107200
  1325.7 33.3 %reshape.240 = f32[4,1,409600]{2,1,0:T(1,128)} reshape(f32[160,2,4,32,40]{4,3,2,1,0:T(8,128)} %bitcast.111) | data formatting | bytes 13107200
  1408.9 50.6 %all-to-all-done.3 = f32[4,1,409600]{2,1,0:T(1,128)} async-done(((f32[4,1,409600]{2,1,0:T(1,128)}), f32[4,1,409600]{2,1,0:T(1,128)}, u32[]{:S(2)}, u32[]{:S(2)}) %all-to-all-start.3) | async-done | bytes 6553632 | tf_op jit(solution)/shard_map/all_to_all | solution.py:64
  1488.3 120.7 %all-to-all-done.8 = f32[8,1,204800]{2,1,0:T(1,128)} async-done(((f32[8,1,204800]{2,1,0:T(1,128)}), f32[8,1,204800]{2,1,0:T(1,128)}, u32[]{:S(2)}, u32[]{:S(2)}) %all-to-all-start.8) | async-done | bytes 6553632 | tf_op jit(solution)/shard_map/all_to_all | solution.py:60
  1614.2 71.4 %reduce.3 = f32[4,409600]{1,0:T(4,128)} reduce(f32[4,1,409600]{2,1,0:T(1,128)} %all-to-all-done.9, f32[]{:T(128)} %broadcast.227), dimensions={1}, to_apply=%all_to_all.173.reduce_sub_computation | reduce | bytes 13107204 | tf_op jit(solution)/shard_map/all_to_all | solution.py:78
  1685.6 27.3 reshape.227
  1712.9 25.6 copy.191
  1738.4 30.3 %copy.179 = f32[2,4,40,4,40,32]{4,5,3,0,2,1:T(8,128)} copy(f32[2,4,40,4,40,32]{2,1,5,4,3,0:T(4,128)} %bitcast.128) | data formatting | bytes 13107200 | tf_op jit(solution)/shard_map/all_to_all | solution.py:78
  1797.6 71.7 %reduce.6 = f32[4,409600]{1,0:T(4,128)} reduce(f32[4,1,409600]{2,1,0:T(1,128)} %all-to-all-done.6, f32[]{:T(128)} %broadcast.227), dimensions={1}, to_apply=%all_to_all.162.reduce_sub_computation | reduce | bytes 13107204 | tf_op jit(solution)/shard_map/all_to_all | solution.py:71
  1869.4 27.3 reshape.233
  1896.7 25.6 copy.192
  1922.3 30.2 %copy.177 = f32[2,4,40,4,40,32]{4,5,3,0,2,1:T(8,128)} copy(f32[2,4,40,4,40,32]{2,1,5,4,3,0:T(4,128)} %bitcast.131) | data formatting | bytes 13107200 | tf_op jit(solution)/shard_map/all_to_all | solution.py:71
  1981.4 71.8 %reduce.9 = f32[4,409600]{1,0:T(4,128)} reduce(f32[4,1,409600]{2,1,0:T(1,128)} %all-to-all-done.3, f32[]{:T(128)} %broadcast.227), dimensions={1}, to_apply=%all_to_all.150.reduce_sub_computation | reduce | bytes 13107204 | tf_op jit(solution)/shard_map/all_to_all | solution.py:64
  2053.2 27.3 reshape.241
  2080.5 25.6 copy.193
  2106.0 30.3 %copy.174 = f32[2,4,40,4,40,32]{4,5,3,0,2,1:T(8,128)} copy(f32[2,4,40,4,40,32]{2,1,5,4,3,0:T(4,128)} %bitcast.134) | data formatting | bytes 13107200 | tf_op jit(solution)/shard_map/all_to_all | solution.py:64
  2167.2 57.2 %reduce.2 = f32[8,204800]{1,0:T(8,128)} reduce(f32[8,1,204800]{2,1,0:T(1,128)} %all-to-all-done.8, f32[]{:T(128)} %broadcast.227), dimensions={1}, to_apply=%all_to_all.170.reduce_sub_computation | reduce | bytes 13107204 | tf_op jit(solution)/shard_map/all_to_all | solution.py:60
  2224.3 26.7 reshape.225
  2290.7 57.2 %reduce.8 = f32[8,204800]{1,0:T(8,128)} reduce(f32[8,1,204800]{2,1,0:T(1,128)} %all-to-all-done.2, f32[]{:T(128)} %broadcast.227), dimensions={1}, to_apply=%all_to_all.147.reduce_sub_computation | reduce | bytes 13107204 | tf_op jit(solution)/shard_map/all_to_all | solution.py:59
  2347.9 26.7 reshape.239
  2458.9 57.0 %reduce.4 = f32[8,204800]{1,0:T(8,128)} reduce(f32[8,1,204800]{2,1,0:T(1,128)} %all-to-all-done.10, f32[]{:T(128)} %broadcast.227), dimensions={1}, to_apply=%all_to_all.177.reduce_sub_computation | reduce | bytes 13107204 | tf_op jit(solution)/shard_map/all_to_all | solution.py:77
  2515.9 27.0 reshape.229
  2542.9 23.6 copy.163
  2566.5 57.0 %reduce.7 = f32[8,204800]{1,0:T(8,128)} reduce(f32[8,1,204800]{2,1,0:T(1,128)} %all-to-all-done.7, f32[]{:T(128)} %broadcast.227), dimensions={1}, to_apply=%all_to_all.166.reduce_sub_computation | reduce | bytes 13107204 | tf_op jit(solution)/shard_map/all_to_all | solution.py:70
  2623.4 26.8 reshape.235
  2650.2 23.5 copy.155
  2673.7 57.2 %reduce.10 = f32[8,204800]{1,0:T(8,128)} reduce(f32[8,1,204800]{2,1,0:T(1,128)} %all-to-all-done.4, f32[]{:T(128)} %broadcast.227), dimensions={1}, to_apply=%all_to_all.154.reduce_sub_computation | reduce | bytes 13107204 | tf_op jit(solution)/shard_map/all_to_all | solution.py:63
  2730.9 26.7 reshape.243
  2757.7 23.6 copy.146
  2781.2 65.5 %fusion.9 = (f32[1,40,32,20,32]{2,1,3,4,0:T(8,128)}, f32[1,40,32,20,32]{2,1,3,4,0:T(8,128)}) fusion(f32[2,40,32,20,32]{2,1,3,4,0:T(8,128)} %slice_bitcast_fusion, f32[1,40,32,20,32]{2,1,3,4,0:T(8,128)} %copy.164, f32[2,40,32,20,32]{2,1,3,4,0:T(8,128)} %bitcast.114, f32[2,40,32,20,32]{2,1,3,4,0:T(8,128)} %bitcast.115, ...), kind=kLoop, calls=%fused_computation.23 | loop fusion | flops 18841600 | bytes 52443392 | tf_op jit(solution)/shard_map/sub | solution.py:96
  (99 shorter events, 579.7 us)
Async XLA Ops:
  205.9 159.0 %copy-start = (f32[25600]{0:T(1024)}, f32[25600]{0:T(1024)S(1)}, u32[]{:S(2)}) copy-start(f32[25600]{0:T(1024)S(1)} %gather_fusion.1) | copy-start | bytes 307204
  206.7 158.2 %copy-start.8 = (f32[20,160]{1,0:T(8,128)S(1)}, f32[20,160]{1,0:T(8,128)}, u32[]{:S(2)}) copy-start(f32[20,160]{1,0:T(8,128)} %param.3) | copy-start | bytes 38404
  364.8 75.4 %copy-start.2 = (f32[25600]{0:T(1024)}, f32[25600]{0:T(1024)S(1)}, u32[]{:S(2)}) copy-start(f32[25600]{0:T(1024)S(1)} %gather_fusion) | copy-start | bytes 307204
  530.5 151.2 %all-to-all-start = ((f32[8,1,204800]{2,1,0:T(1,128)}), f32[8,1,204800]{2,1,0:T(1,128)}, u32[]{:S(2)}, u32[]{:S(2)}) async-start(f32[8,1,204800]{2,1,0:T(1,128)} %reshape.236), calls=%async_computation | async-start | bytes 13107200 | tf_op jit(solution)/shard_map/all_to_all | solution.py:53
  681.7 147.7 %all-to-all-start.1 = ((f32[8,1,204800]{2,1,0:T(1,128)}), f32[8,1,204800]{2,1,0:T(1,128)}, u32[]{:S(2)}, u32[]{:S(2)}) async-start(f32[8,1,204800]{2,1,0:T(1,128)} %reshape.222), calls=%async_computation.1 | async-start | bytes 13107200 | tf_op jit(solution)/shard_map/all_to_all | solution.py:52
  733.6 100.6 %copy-start.1 = (f32[25600]{0:T(1024)S(1)}, f32[25600]{0:T(1024)}, u32[]{:S(2)}) copy-start(f32[25600]{0:T(1024)} %copy-done) | copy-start | bytes 307204
  733.6 100.7 %copy-start.3 = (f32[25600]{0:T(1024)S(1)}, f32[25600]{0:T(1024)}, u32[]{:S(2)}) copy-start(f32[25600]{0:T(1024)} %copy-done.2) | copy-start | bytes 307204
  829.4 332.5 %all-to-all-start.5 = ((f32[8,1,204800]{2,1,0:T(1,128)}), f32[8,1,204800]{2,1,0:T(1,128)}, u32[]{:S(2)}, u32[]{:S(2)}) async-start(f32[8,1,204800]{2,1,0:T(1,128)} %reshape.230), calls=%async_computation.5 | async-start | bytes 13107200 | tf_op jit(solution)/shard_map/all_to_all | solution.py:54
  1039.3 53.7 %slice-start = ((s8[10485760]{0:T(1024)(128)(4,1)}), s8[4194304]{0:T(1024)(128)(4,1)S(1)}, s32[]{:S(2)}) async-start(s8[10485760]{0:T(1024)(128)(4,1)} %bitcast.146), calls=%async_computation.11 | async-start | bytes 8388608
  1039.3 53.7 %slice-start.1 = ((s8[10485760]{0:T(1024)(128)(4,1)}), s8[4194304]{0:T(1024)(128)(4,1)S(1)}, s32[]{:S(2)}) async-start(s8[10485760]{0:T(1024)(128)(4,1)} %bitcast.146), calls=%async_computation.12 | async-start | bytes 8388608
  1049.4 43.6 %slice-start.2 = ((s8[10485760]{0:T(1024)(128)(4,1)}), s8[2097152]{0:T(1024)(128)(4,1)S(1)}, s32[]{:S(2)}) async-start(s8[10485760]{0:T(1024)(128)(4,1)} %bitcast.146), calls=%async_computation.13 | async-start | bytes 4194304
  1161.8 139.8 %all-to-all-start.9 = ((f32[4,1,409600]{2,1,0:T(1,128)}), f32[4,1,409600]{2,1,0:T(1,128)}, u32[]{:S(2)}, u32[]{:S(2)}) async-start(f32[4,1,409600]{2,1,0:T(1,128)} %reshape.226), calls=%async_computation.9 | async-start | bytes 13107200 | tf_op jit(solution)/shard_map/all_to_all | solution.py:78
  1301.6 79.0 %all-to-all-start.6 = ((f32[4,1,409600]{2,1,0:T(1,128)}), f32[4,1,409600]{2,1,0:T(1,128)}, u32[]{:S(2)}, u32[]{:S(2)}) async-start(f32[4,1,409600]{2,1,0:T(1,128)} %reshape.232), calls=%async_computation.6 | async-start | bytes 13107200 | tf_op jit(solution)/shard_map/all_to_all | solution.py:71
  1380.6 78.8 %all-to-all-start.3 = ((f32[4,1,409600]{2,1,0:T(1,128)}), f32[4,1,409600]{2,1,0:T(1,128)}, u32[]{:S(2)}, u32[]{:S(2)}) async-start(f32[4,1,409600]{2,1,0:T(1,128)} %reshape.240), calls=%async_computation.3 | async-start | bytes 13107200 | tf_op jit(solution)/shard_map/all_to_all | solution.py:64
  1459.4 149.5 %all-to-all-start.8 = ((f32[8,1,204800]{2,1,0:T(1,128)}), f32[8,1,204800]{2,1,0:T(1,128)}, u32[]{:S(2)}, u32[]{:S(2)}) async-start(f32[8,1,204800]{2,1,0:T(1,128)} %reshape.224), calls=%async_computation.8 | async-start | bytes 13107200 | tf_op jit(solution)/shard_map/all_to_all | solution.py:60
  1609.0 182.7 %all-to-all-start.2 = ((f32[8,1,204800]{2,1,0:T(1,128)}), f32[8,1,204800]{2,1,0:T(1,128)}, u32[]{:S(2)}, u32[]{:S(2)}) async-start(f32[8,1,204800]{2,1,0:T(1,128)} %reshape.238), calls=%async_computation.2 | async-start | bytes 13107200 | tf_op jit(solution)/shard_map/all_to_all | solution.py:59
  1791.6 183.7 %all-to-all-start.10 = ((f32[8,1,204800]{2,1,0:T(1,128)}), f32[8,1,204800]{2,1,0:T(1,128)}, u32[]{:S(2)}, u32[]{:S(2)}) async-start(f32[8,1,204800]{2,1,0:T(1,128)} %reshape.228), calls=%async_computation.10 | async-start | bytes 13107200 | tf_op jit(solution)/shard_map/all_to_all | solution.py:77
  1975.4 183.9 %all-to-all-start.7 = ((f32[8,1,204800]{2,1,0:T(1,128)}), f32[8,1,204800]{2,1,0:T(1,128)}, u32[]{:S(2)}, u32[]{:S(2)}) async-start(f32[8,1,204800]{2,1,0:T(1,128)} %reshape.234), calls=%async_computation.7 | async-start | bytes 13107200 | tf_op jit(solution)/shard_map/all_to_all | solution.py:70
  2159.3 514.5 %all-to-all-start.4 = ((f32[8,1,204800]{2,1,0:T(1,128)}), f32[8,1,204800]{2,1,0:T(1,128)}, u32[]{:S(2)}, u32[]{:S(2)}) async-start(f32[8,1,204800]{2,1,0:T(1,128)} %reshape.242), calls=%async_computation.4 | async-start | bytes 13107200 | tf_op jit(solution)/shard_map/all_to_all | solution.py:63
  2757.6 23.6 copy-start.4
  2757.6 23.6 copy-start.5
  2757.6 23.6 copy-start.6
  2757.6 23.6 copy-start.7
where the time goes:
time: 2910 us; the launch traced here: 2900 us
  local copies, waits for them, and re-layouts  1540 us (53%)
  other arithmetic  810 us (28%)
  waiting for transfers between devices  368 us (13%)
  matrix products  119 us (4%)
  starting transfers between devices  62.1 us (2%)
    unnamed x47, local copies, waits for them, and re-layouts  627 us
    gather x6, local copies, waits for them, and re-layouts, operators(): return (kinetic_row[distance], slope_row[distance])  317 us
    all_to_all x1, waiting for transfers between devices, on_device(): lax.all_to_all(grad_two, 'row', split_axis=3, concat_axis=2, tiled=True)  121 us
    all_to_all x1, waiting for transfers between devices, on_device(): lax.all_to_all(window_part, 'row', split_axis=2, concat_axis=3, tiled=True)  95.8 us
    all_to_all x1, waiting for transfers between devices, on_device(): lax.all_to_all(applied, 'row', split_axis=2, concat_axis=3, tiled=True)  79.3 us
    dot_general x1, matrix products, on_device(): jnp.einsum('cpqbx,xe->cpebq', density, matrices, precision=highest)  75.3 us
    all_to_all x1, other arithmetic, on_device(): lax.all_to_all(full_applied, 'col', split_axis=3, concat_axis=1, tiled=True)  71.8 us
    all_to_all x1, other arithmetic, on_device(): lax.all_to_all(grad_mid, 'col', split_axis=3, concat_axis=1, tiled=True)  71.7 us
  transfers between devices with their start and end apart: 11, of which 5 were waited for; matrix products, arithmetic and copies ran while one was open for 59% of the time, Pallas kernels for 0%

commit v1 on v0

--- a/solution.py
+++ b/solution.py
@@ -6,6 +6,17 @@
 friction = 0.005
 diffusion = 0.0001
 highest = lax.Precision.HIGHEST
+
+
+def cut_along(x, dim, devices):
+    before, after = (x.shape[:dim], x.shape[dim + 1 :])
+    return jnp.moveaxis(x.reshape(*before, devices, -1, *after), dim, 0)
+
+
+def laid_out(tiles, dim):
+    shape = list(tiles.shape[1:])
+    shape[dim] *= tiles.shape[0]
+    return jnp.moveaxis(tiles, 0, dim).reshape(shape)
 
 
 def operators(grid_width):
@@ -50,7 +61,14 @@
     offset_two = rows_global - cols_global
     squared = offset_one**2 + offset_two**2
     source = lax.all_to_all(window_part, "row", split_axis=2, concat_axis=3, tiled=True)
-    applied_mid = lax.all_to_all(applied, "row", split_axis=2, concat_axis=3, tiled=True)
+    length, here = (lax.axis_size("row"), lax.axis_index("row"))
+    blocks = cut_along(applied, 2, length)
+    done = [blocks[here]]
+    for step in range(1, length):
+        sent = blocks[here ^ step]
+        done.append(lax.ppermute(sent, "row", [(i, i ^ step) for i in range(length)]))
+    blocks = jnp.stack(done)[here ^ jnp.arange(length)]
+    applied_mid = laid_out(blocks, 3)
     grad_mid = lax.all_to_all(grad_one, "row", split_axis=2, concat_axis=3, tiled=True)
     paired = jnp.einsum("capbq,eb->capeq", source, stacked, precision=highest)
     full_applied = applied_mid + paired[:, :, :, :grid_width]

time: 2910 us -> 3210 us (1.10)
  waiting for transfers between devices: 368 us -> 577 us
  starting transfers between devices: 62.1 us -> 189 us
  other arithmetic: 810 us -> 754 us
    ppermute x0 -> x7, waiting for transfers between devices: none -> 384 us  [on_device(): lax.ppermute(sent, 'row', [(i, i ^ step) for i in range(length)])]
    all_to_all x1, starting transfers between devices: 5.9 us -> 108 us  [on_device(): lax.all_to_all(grad_two, 'row', split_axis=3, concat_axis=2, tiled=True)]
    all_to_all x1, waiting for transfers between devices: 95.8 us -> 0.01 us  [on_device(): lax.all_to_all(window_part, 'row', split_axis=2, concat_axis=3, tiled=True)]
    all_to_all x1 -> x0, waiting for transfers between devices: 79.3 us -> none  [on_device(): lax.all_to_all(applied, 'row', split_axis=2, concat_axis=3, tiled=True)]
    all_to_all x1 -> x0, other arithmetic: 57 us -> none  [on_device(): lax.all_to_all(applied, 'row', split_axis=2, concat_axis=3, tiled=True)]
    all_to_all x3 -> x0, local copies, waits for them, and re-layouts: 36.9 us -> none  [on_device(): lax.all_to_all(applied, 'row', split_axis=2, concat_axis=3, tiled=True)]
    unnamed x47 -> x48, local copies, waits for them, and re-layouts: 627 us -> 599 us
  transfers between devices with their start and end apart: 11 -> 17, of which waited for: 5 -> 7; matrix products, arithmetic and copies ran while one was open for 59% -> 66% of each run, Pallas kernels for 0% -> 0%
where the time goes in v1:
time: 3210 us; the launch traced here: 3200 us
  local copies, waits for them, and re-layouts  1560 us (49%)
  other arithmetic  754 us (23%)
  waiting for transfers between devices  577 us (18%)
  starting transfers between devices  189 us (6%)
  matrix products  118 us (4%)
    unnamed x48, local copies, waits for them, and re-layouts  599 us
    ppermute x7, waiting for transfers between devices, on_device(): lax.ppermute(sent, 'row', [(i, i ^ step) for i in range(length)])  384 us
    gather x6, local copies, waits for them, and re-layouts, operators(): return (kinetic_row[distance], slope_row[distance])  317 us
    all_to_all x1, waiting for transfers between devices, on_device(): lax.all_to_all(grad_two, 'row', split_axis=3, concat_axis=2, tiled=True)  121 us
    all_to_all x1, starting transfers between devices, on_device(): lax.all_to_all(grad_two, 'row', split_axis=3, concat_axis=2, tiled=True)  108 us
    dot_general x1, matrix products, on_device(): jnp.einsum('cpqbx,xe->cpebq', density, matrices, precision=highest)  74.8 us
    all_to_all x1, other arithmetic, on_device(): lax.all_to_all(full_applied, 'col', split_axis=3, concat_axis=1, tiled=True)  71.6 us
    all_to_all x1, other arithmetic, on_device(): lax.all_to_all(grad_mid, 'col', split_axis=3, concat_axis=1, tiled=True)  71.6 us
  transfers between devices with their start and end apart: 17, of which 7 were waited for; matrix products, arithmetic and copies ran while one was open for 66% of the time, Pallas kernels for 0%

profile of v1, /device:TPU:0, one launch (start us, length us, event | category | flops | bytes accessed | tf_op | source)
XLA Modules:
  0.0 3195.2 jit_solution(15052647901109874781)
XLA Ops:
  0.0 46.7 %copy.148 = f32[2,40,32,20,160]{4,1,3,2,0:T(8,128)} copy(f32[2,40,32,20,160]{4,2,3,1,0:T(8,128)} %param.2) | data formatting | bytes 65536000 | tf_op args[0]
  64.3 24.2 copy.162
  120.3 158.1 %gather_fusion.1 = f32[25600]{0:T(1024)S(1)} fusion(f32[160]{0:T(256)S(1)} %negate_multiply_fusion, s32[25600]{0:T(1024)S(1)} %broadcast_clamp_fusion), kind=kCustom, calls=%fused_computation.1 | custom fusion | bytes 307200 | tf_op jit(solution)/shard_map/gather | solution.py:32
  279.2 158.1 %gather_fusion = f32[25600]{0:T(1024)S(1)} fusion(f32[160]{0:T(256)S(1)} %broadcast_multiply_fusion, s32[25600]{0:T(1024)S(1)} %broadcast_clamp_fusion), kind=kCustom, calls=%fused_computation | custom fusion | bytes 307200 | tf_op jit(solution)/shard_map/gather | solution.py:32
  437.5 74.8 %convolution_bitcast_fusion = f32[2,40,64,20,32]{2,1,3,4,0:T(8,128)} fusion(f32[160,32]{0,1:T(8,128)S(1)} %bitcast.186, f32[160,32]{0,1:T(8,128)S(1)} %bitcast.187, f32[2,40,32,20,160]{4,2,3,1,0:T(8,128)} %param.2), kind=kOutput, calls=%fused_computation.11 | convolution fusion | flops 6291466240 | bytes 45916160 | tf_op jit(solution)/shard_map/cpqbx,xe->cpebq/dot_general | solution.py:42
  512.3 43.2 %slice_add_fusion = (f32[2,40,32,20,32]{2,1,3,4,0:T(8,128)}, f32[2,40,32,20,32]{2,1,3,4,0:T(8,128)}) fusion(f32[2,40,64,20,32]{2,1,3,4,0:T(8,128)} %convolution_bitcast_fusion, f32[32,20]{0,1:T(8,128)S(1)} %slice_bitcast_fusion.1, f32[2,40,32,20,160]{4,1,3,2,0:T(8,128)} %copy.148), kind=kLoop, calls=%fused_computation.4 | loop fusion | flops 3276800 | bytes 32770560 | tf_op jit(solution)/shard_map/add | solution.py:47
  555.5 24.2 copy.176
  608.6 24.2 copy.150
  672.7 66.9 %collective-permute-done = f32[2,40,4,20,32]{1,4,2,3,0:T(8,128)} collective-permute-done((f32[2,40,4,20,32]{1,4,2,3,0:T(8,128)}, f32[2,40,4,20,32]{1,4,2,3,0:T(8,128)}, u32[]{:S(2)}, u32[]{:S(2)}) %collective-permute-start) | collective-permute-done | bytes 819232 | tf_op jit(solution)/shard_map/ppermute | solution.py:69
  760.5 91.9 %collective-permute-done.1 = f32[2,40,4,20,32]{1,4,2,3,0:T(8,128)} collective-permute-done((f32[2,40,4,20,32]{1,4,2,3,0:T(8,128)}, f32[2,40,4,20,32]{1,4,2,3,0:T(8,128)}, u32[]{:S(2)}, u32[]{:S(2)}) %collective-permute-start.1) | collective-permute-done | bytes 819232 | tf_op jit(solution)/shard_map/ppermute | solution.py:69
  858.7 48.7 %collective-permute-done.2 = f32[2,40,4,20,32]{1,4,2,3,0:T(8,128)} collective-permute-done((f32[2,40,4,20,32]{1,4,2,3,0:T(8,128)}, f32[2,40,4,20,32]{1,4,2,3,0:T(8,128)}, u32[]{:S(2)}, u32[]{:S(2)}) %collective-permute-start.2) | collective-permute-done | bytes 819232 | tf_op jit(solution)/shard_map/ppermute | solution.py:69
  914.8 176.2 %collective-permute-done.4 = f32[2,40,4,20,32]{1,4,2,3,0:T(8,128)} collective-permute-done((f32[2,40,4,20,32]{1,4,2,3,0:T(8,128)}, f32[2,40,4,20,32]{1,4,2,3,0:T(8,128)}, u32[]{:S(2)}, u32[]{:S(2)}) %collective-permute-start.4) | collective-permute-done | bytes 819232 | tf_op jit(solution)/shard_map/ppermute | solution.py:69
  1151.3 57.3 %reduce = f32[8,204800]{1,0:T(8,128)} reduce(f32[8,1,204800]{2,1,0:T(1,128)} %all-to-all-done, f32[]{:T(128)} %broadcast.262), dimensions={1}, to_apply=%all_to_all.126.reduce_sub_computation | reduce | bytes 13107204 | tf_op jit(solution)/shard_map/all_to_all | solution.py:63
  1208.6 26.6 reshape.270
  1245.3 43.6 %fusion.15 = f32[2,40,4,320,32]{3,1,4,2,0:T(8,128)} fusion(f32[2,40,4,160,32]{1,4,3,2,0:T(8,128)S(1)} %bitcast.149, f32[160,160]{0,1:T(8,128)S(1)} %copy.161, f32[160,160]{0,1:T(8,128)S(1)} %copy.160), kind=kOutput, calls=%fused_computation.35 | convolution fusion | flops 6291507200 | bytes 19865600 | tf_op jit(solution)/shard_map/capbq,eb->capeq/dot_general | solution.py:73
  1324.2 33.7 %reshape.273 = f32[4,1,409600]{2,1,0:T(1,128)} reshape(f32[160,2,4,32,40]{4,3,2,1,0:T(8,128)} %bitcast.145) | data formatting | bytes 13107200
  1363.3 57.0 %reduce.4 = f32[8,204800]{1,0:T(8,128)} reduce(f32[8,1,204800]{2,1,0:T(1,128)} %all-to-all-done.4, f32[]{:T(128)} %broadcast.262), dimensions={1}, to_apply=%all_to_all.141.reduce_sub_computation | reduce | bytes 13107204 | tf_op jit(solution)/shard_map/all_to_all | solution.py:72
  1420.2 26.7 reshape.278
  1464.2 33.4 %reshape.279 = f32[4,1,409600]{2,1,0:T(1,128)} reshape(f32[160,2,4,32,40]{4,3,2,1,0:T(8,128)} %bitcast.162) | data formatting | bytes 13107200
  1522.0 33.4 %reshape.285 = f32[4,1,409600]{2,1,0:T(1,128)} reshape(f32[160,2,4,32,40]{4,3,2,1,0:T(8,128)} %bitcast.147) | data formatting | bytes 13107200
  1605.1 50.6 %all-to-all-done.2 = f32[4,1,409600]{2,1,0:T(1,128)} async-done(((f32[4,1,409600]{2,1,0:T(1,128)}), f32[4,1,409600]{2,1,0:T(1,128)}, u32[]{:S(2)}, u32[]{:S(2)}) %all-to-all-start.2) | async-done | bytes 6553632 | tf_op jit(solution)/shard_map/all_to_all | solution.py:82
  1655.7 108.5 %all-to-all-start.7 = ((f32[8,1,204800]{2,1,0:T(1,128)}), f32[8,1,204800]{2,1,0:T(1,128)}, u32[]{:S(2)}, u32[]{:S(2)}) async-start(f32[8,1,204800]{2,1,0:T(1,128)} %reshape.271), calls=%async_computation.7 | async-start | bytes 13107200 | tf_op jit(solution)/shard_map/all_to_all | solution.py:78
  1787.1 121.3 %all-to-all-done.7 = f32[8,1,204800]{2,1,0:T(1,128)} async-done(((f32[8,1,204800]{2,1,0:T(1,128)}), f32[8,1,204800]{2,1,0:T(1,128)}, u32[]{:S(2)}, u32[]{:S(2)}) %all-to-all-start.7) | async-done | bytes 6553632 | tf_op jit(solution)/shard_map/all_to_all | solution.py:78
  1913.3 71.5 %reduce.2 = f32[4,409600]{1,0:T(4,128)} reduce(f32[4,1,409600]{2,1,0:T(1,128)} %all-to-all-done.8, f32[]{:T(128)} %broadcast.262), dimensions={1}, to_apply=%all_to_all.156.reduce_sub_computation | reduce | bytes 13107204 | tf_op jit(solution)/shard_map/all_to_all | solution.py:96
  1984.8 27.5 reshape.274
  2012.3 25.6 copy.226
  2037.9 30.3 copy.206
  2097.1 71.6 %reduce.5 = f32[4,409600]{1,0:T(4,128)} reduce(f32[4,1,409600]{2,1,0:T(1,128)} %all-to-all-done.5, f32[]{:T(128)} %broadcast.262), dimensions={1}, to_apply=%all_to_all.145.reduce_sub_computation | reduce | bytes 13107204 | tf_op jit(solution)/shard_map/all_to_all | solution.py:89
  2168.7 27.5 reshape.280
  2196.2 25.6 copy.227
  2221.8 30.2 copy.204
  2280.9 71.6 %reduce.8 = f32[4,409600]{1,0:T(4,128)} reduce(f32[4,1,409600]{2,1,0:T(1,128)} %all-to-all-done.2, f32[]{:T(128)} %broadcast.262), dimensions={1}, to_apply=%all_to_all.133.reduce_sub_computation | reduce | bytes 13107204 | tf_op jit(solution)/shard_map/all_to_all | solution.py:82
  2352.6 27.5 reshape.286
  2380.1 25.6 copy.228
  2405.7 30.3 copy.201
  2466.8 57.0 %reduce.1 = f32[8,204800]{1,0:T(8,128)} reduce(f32[8,1,204800]{2,1,0:T(1,128)} %all-to-all-done.7, f32[]{:T(128)} %broadcast.262), dimensions={1}, to_apply=%all_to_all.153.reduce_sub_computation | reduce | bytes 13107204 | tf_op jit(solution)/shard_map/all_to_all | solution.py:78
  2523.9 26.7 reshape.272
  2590.1 57.3 %reduce.7 = f32[8,204800]{1,0:T(8,128)} reduce(f32[8,1,204800]{2,1,0:T(1,128)} %all-to-all-done.1, f32[]{:T(128)} %broadcast.262), dimensions={1}, to_apply=%all_to_all.130.reduce_sub_computation | reduce | bytes 13107204 | tf_op jit(solution)/shard_map/all_to_all | solution.py:77
  2647.5 26.6 reshape.284
  2758.5 57.1 %reduce.3 = f32[8,204800]{1,0:T(8,128)} reduce(f32[8,1,204800]{2,1,0:T(1,128)} %all-to-all-done.9, f32[]{:T(128)} %broadcast.262), dimensions={1}, to_apply=%all_to_all.160.reduce_sub_computation | reduce | bytes 13107204 | tf_op jit(solution)/shard_map/all_to_all | solution.py:95
  2815.6 27.0 reshape.276
  2842.6 23.6 copy.191
  2866.2 57.0 %reduce.6 = f32[8,204800]{1,0:T(8,128)} reduce(f32[8,1,204800]{2,1,0:T(1,128)} %all-to-all-done.6, f32[]{:T(128)} %broadcast.262), dimensions={1}, to_apply=%all_to_all.149.reduce_sub_computation | reduce | bytes 13107204 | tf_op jit(solution)/shard_map/all_to_all | solution.py:88
  2923.2 26.8 reshape.282
  2973.5 57.3 %reduce.9 = f32[8,204800]{1,0:T(8,128)} reduce(f32[8,1,204800]{2,1,0:T(1,128)} %all-to-all-done.3, f32[]{:T(128)} %broadcast.262), dimensions={1}, to_apply=%all_to_all.137.reduce_sub_computation | reduce | bytes 13107204 | tf_op jit(solution)/shard_map/all_to_all | solution.py:81
  3030.8 26.7 reshape.288
  3057.5 23.6 copy.174
  3081.1 65.5 %fusion.9 = (f32[1,40,32,20,32]{2,1,3,4,0:T(8,128)}, f32[1,40,32,20,32]{2,1,3,4,0:T(8,128)}) fusion(f32[2,40,32,20,32]{2,1,3,4,0:T(8,128)} %slice_bitcast_fusion, f32[1,40,32,20,32]{2,1,3,4,0:T(8,128)} %copy.192, f32[2,40,32,20,32]{2,1,3,4,0:T(8,128)} %bitcast.151, f32[2,40,32,20,32]{2,1,3,4,0:T(8,128)} %bitcast.152, ...), kind=kLoop, calls=%fused_computation.24 | loop fusion | flops 18841600 | bytes 52443392 | tf_op jit(solution)/shard_map/sub | solution.py:114
  (123 shorter events, 668.4 us)
Async XLA Ops:
  111.4 491.2 %all-to-all-start = ((f32[8,1,204800]{2,1,0:T(1,128)}), f32[8,1,204800]{2,1,0:T(1,128)}, u32[]{:S(2)}, u32[]{:S(2)}) async-start(f32[8,1,204800]{2,1,0:T(1,128)} %reshape.269), calls=%async_computation | async-start | bytes 13107200 | tf_op jit(solution)/shard_map/all_to_all | solution.py:63
  278.4 159.0 %copy-start = (f32[25600]{0:T(1024)}, f32[25600]{0:T(1024)S(1)}, u32[]{:S(2)}) copy-start(f32[25600]{0:T(1024)S(1)} %gather_fusion.1) | copy-start | bytes 307204
  279.2 158.2 %copy-start.6 = (f32[20,160]{1,0:T(8,128)S(1)}, f32[20,160]{1,0:T(8,128)}, u32[]{:S(2)}) copy-start(f32[20,160]{1,0:T(8,128)} %param.3) | copy-start | bytes 38404
  602.6 755.3 %all-to-all-start.4 = ((f32[8,1,204800]{2,1,0:T(1,128)}), f32[8,1,204800]{2,1,0:T(1,128)}, u32[]{:S(2)}, u32[]{:S(2)}) async-start(f32[8,1,204800]{2,1,0:T(1,128)} %reshape.277), calls=%async_computation.4 | async-start | bytes 13107200 | tf_op jit(solution)/shard_map/all_to_all | solution.py:72
  644.5 18.8 copy-start.1
  648.1 91.5 %collective-permute-start = (f32[2,40,4,20,32]{1,4,2,3,0:T(8,128)}, f32[2,40,4,20,32]{1,4,2,3,0:T(8,128)}, u32[]{:S(2)}, u32[]{:S(2)}) collective-permute-start(f32[2,40,4,20,32]{1,4,2,3,0:T(8,128)} %bitcast.143), channel_id=1, source_target_pairs={{0,4},{4,0},{8,12},{12,8},{16,20},{20,16},{24,28},{28,24},{1,5},{5... | collective-permute-start | bytes 2457608 | tf_op jit(solution)/shard_map/ppermute | solution.py:69
  651.9 200.5 %collective-permute-start.1 = (f32[2,40,4,20,32]{1,4,2,3,0:T(8,128)}, f32[2,40,4,20,32]{1,4,2,3,0:T(8,128)}, u32[]{:S(2)}, u32[]{:S(2)}) collective-permute-start(f32[2,40,4,20,32]{1,4,2,3,0:T(8,128)} %bitcast.142), channel_id=1, source_target_pairs={{0,8},{4,12},{8,0},{12,4},{16,24},{20,28},{24,16},{28,20},{1,9},{5... | collective-permute-start | bytes 2457608 | tf_op jit(solution)/shard_map/ppermute | solution.py:69
  655.2 252.2 %collective-permute-start.2 = (f32[2,40,4,20,32]{1,4,2,3,0:T(8,128)}, f32[2,40,4,20,32]{1,4,2,3,0:T(8,128)}, u32[]{:S(2)}, u32[]{:S(2)}) collective-permute-start(f32[2,40,4,20,32]{1,4,2,3,0:T(8,128)} %bitcast.141), channel_id=1, source_target_pairs={{0,12},{4,8},{8,4},{12,0},{16,28},{20,24},{24,20},{28,16},{1,13},{... | collective-permute-start | bytes 2457608 | tf_op jit(solution)/shard_map/ppermute | solution.py:69
  657.0 254.1 %collective-permute-start.3 = (f32[2,40,4,20,32]{1,4,2,3,0:T(8,128)}, f32[2,40,4,20,32]{1,4,2,3,0:T(8,128)}, u32[]{:S(2)}, u32[]{:S(2)}) collective-permute-start(f32[2,40,4,20,32]{1,4,2,3,0:T(8,128)} %bitcast.140), channel_id=1, source_target_pairs={{0,16},{4,20},{8,24},{12,28},{16,0},{20,4},{24,8},{28,12},{1,17},{... | collective-permute-start | bytes 2457608 | tf_op jit(solution)/shard_map/ppermute | solution.py:69
  661.8 429.2 %collective-permute-start.4 = (f32[2,40,4,20,32]{1,4,2,3,0:T(8,128)}, f32[2,40,4,20,32]{1,4,2,3,0:T(8,128)}, u32[]{:S(2)}, u32[]{:S(2)}) collective-permute-start(f32[2,40,4,20,32]{1,4,2,3,0:T(8,128)} %bitcast.139), channel_id=1, source_target_pairs={{0,20},{4,16},{8,28},{12,24},{16,4},{20,0},{24,12},{28,8},{1,21},{... | collective-permute-start | bytes 2457608 | tf_op jit(solution)/shard_map/ppermute | solution.py:69
  739.6 355.0 %collective-permute-start.5 = (f32[2,40,4,20,32]{1,4,2,3,0:T(8,128)}, f32[2,40,4,20,32]{1,4,2,3,0:T(8,128)S(1)}, u32[]{:S(2)}, u32[]{:S(2)}) collective-permute-start(f32[2,40,4,20,32]{1,4,2,3,0:T(8,128)} %bitcast.185), channel_id=1, source_target_pairs={{0,24},{4,28},{8,16},{12,20},{16,8},{20,12},{24,0},{28,4},{1,25},{... | collective-permute-start | bytes 2457608 | tf_op jit(solution)/shard_map/ppermute | solution.py:69
  852.4 243.9 %collective-permute-start.6 = (f32[2,40,4,20,32]{1,4,2,3,0:T(8,128)}, f32[2,40,4,20,32]{1,4,2,3,0:T(8,128)S(1)}, u32[]{:S(2)}, u32[]{:S(2)}) collective-permute-start(f32[2,40,4,20,32]{1,4,2,3,0:T(8,128)} %bitcast.184), channel_id=1, source_target_pairs={{0,28},{4,24},{8,20},{12,16},{16,12},{20,8},{24,4},{28,0},{1,29},{... | collective-permute-start | bytes 2457608 | tf_op jit(solution)/shard_map/ppermute | solution.py:69
  1235.3 53.7 %slice-start = ((s8[10485760]{0:T(1024)(128)(4,1)}), s8[4194304]{0:T(1024)(128)(4,1)S(1)}, s32[]{:S(2)}) async-start(s8[10485760]{0:T(1024)(128)(4,1)} %bitcast.182), calls=%async_computation.10 | async-start | bytes 8388608
  1235.3 53.7 %slice-start.1 = ((s8[10485760]{0:T(1024)(128)(4,1)}), s8[4194304]{0:T(1024)(128)(4,1)S(1)}, s32[]{:S(2)}) async-start(s8[10485760]{0:T(1024)(128)(4,1)} %bitcast.182), calls=%async_computation.11 | async-start | bytes 8388608
  1245.3 43.6 %slice-start.2 = ((s8[10485760]{0:T(1024)(128)(4,1)}), s8[2097152]{0:T(1024)(128)(4,1)S(1)}, s32[]{:S(2)}) async-start(s8[10485760]{0:T(1024)(128)(4,1)} %bitcast.182), calls=%async_computation.12 | async-start | bytes 4194304
  1357.9 139.7 %all-to-all-start.8 = ((f32[4,1,409600]{2,1,0:T(1,128)}), f32[4,1,409600]{2,1,0:T(1,128)}, u32[]{:S(2)}, u32[]{:S(2)}) async-start(f32[4,1,409600]{2,1,0:T(1,128)} %reshape.273), calls=%async_computation.8 | async-start | bytes 13107200 | tf_op jit(solution)/shard_map/all_to_all | solution.py:96
  1497.6 79.2 %all-to-all-start.5 = ((f32[4,1,409600]{2,1,0:T(1,128)}), f32[4,1,409600]{2,1,0:T(1,128)}, u32[]{:S(2)}, u32[]{:S(2)}) async-start(f32[4,1,409600]{2,1,0:T(1,128)} %reshape.279), calls=%async_computation.5 | async-start | bytes 13107200 | tf_op jit(solution)/shard_map/all_to_all | solution.py:89
  1576.8 78.8 %all-to-all-start.2 = ((f32[4,1,409600]{2,1,0:T(1,128)}), f32[4,1,409600]{2,1,0:T(1,128)}, u32[]{:S(2)}, u32[]{:S(2)}) async-start(f32[4,1,409600]{2,1,0:T(1,128)} %reshape.285), calls=%async_computation.2 | async-start | bytes 13107200 | tf_op jit(solution)/shard_map/all_to_all | solution.py:82
  1655.7 252.7 %all-to-all-start.7 = ((f32[8,1,204800]{2,1,0:T(1,128)}), f32[8,1,204800]{2,1,0:T(1,128)}, u32[]{:S(2)}, u32[]{:S(2)}) async-start(f32[8,1,204800]{2,1,0:T(1,128)} %reshape.271), calls=%async_computation.7 | async-start | bytes 13107200 | tf_op jit(solution)/shard_map/all_to_all | solution.py:78
  1908.4 182.8 %all-to-all-start.1 = ((f32[8,1,204800]{2,1,0:T(1,128)}), f32[8,1,204800]{2,1,0:T(1,128)}, u32[]{:S(2)}, u32[]{:S(2)}) async-start(f32[8,1,204800]{2,1,0:T(1,128)} %reshape.283), calls=%async_computation.1 | async-start | bytes 13107200 | tf_op jit(solution)/shard_map/all_to_all | solution.py:77
  2091.2 183.8 %all-to-all-start.9 = ((f32[8,1,204800]{2,1,0:T(1,128)}), f32[8,1,204800]{2,1,0:T(1,128)}, u32[]{:S(2)}, u32[]{:S(2)}) async-start(f32[8,1,204800]{2,1,0:T(1,128)} %reshape.275), calls=%async_computation.9 | async-start | bytes 13107200 | tf_op jit(solution)/shard_map/all_to_all | solution.py:95
  2274.9 184.0 %all-to-all-start.6 = ((f32[8,1,204800]{2,1,0:T(1,128)}), f32[8,1,204800]{2,1,0:T(1,128)}, u32[]{:S(2)}, u32[]{:S(2)}) async-start(f32[8,1,204800]{2,1,0:T(1,128)} %reshape.281), calls=%async_computation.6 | async-start | bytes 13107200 | tf_op jit(solution)/shard_map/all_to_all | solution.py:88
  2458.9 514.6 %all-to-all-start.3 = ((f32[8,1,204800]{2,1,0:T(1,128)}), f32[8,1,204800]{2,1,0:T(1,128)}, u32[]{:S(2)}, u32[]{:S(2)}) async-start(f32[8,1,204800]{2,1,0:T(1,128)} %reshape.287), calls=%async_computation.3 | async-start | bytes 13107200 | tf_op jit(solution)/shard_map/all_to_all | solution.py:81
  3057.5 23.6 copy-start.2
  3057.5 23.6 copy-start.3
  3057.5 23.6 copy-start.4
  3057.5 23.6 copy-start.5
